TPU v7x, 32 devices: a whole 2x2x4 slice. The times are simulated.
32 devices in a mesh: context: 2 (over x), tensor: 4 (over z), dp: 4 (over y, core).
Axes of the slice: x: 2, y: 2, z: 4, core: 2. Of those that a mesh axis runs over, the one named last changes fastest.
Arguments:
- grad_out: bfloat16 [4, 512, 1024], P('dp', 'context', 'tensor'), may hold values from -6 to 6
- inputs: bfloat16 [4, 512, 1024], P('dp', 'context', 'tensor'), may hold values from -0.125 to 0.125
- filt: bfloat16 [512, 1024], P('context', 'tensor'), may hold values from -0.25 to 0.25
Outputs:
- input_grad: bfloat16 [4, 512, 1024], P('dp', 'context', 'tensor')
- filter_grad: float32 [512, 1024], P('context', 'tensor')
All inputs are finite; a program needn't handle non-finite values.
Results may differ from a plain program's by a relative error of at most 0.001.
Values may be sent and summed in bfloat16 or wider, within the bound.
A program may use at most 64 MiB of HBM per device.

v0:
```python
import functools
import math

import jax
import jax.numpy as jnp
import ml_dtypes
import numpy as np
from jax import lax
from jax.experimental import pallas as pl
from jax.experimental.pallas import tpu as pltpu
from jax.sharding import PartitionSpec as P

MESH = pl.DeviceIdType.MESH
NT = (((1,), (1,)), ((), ()))


def half_step_table(n):
    k = np.concatenate([np.arange(0, n, 2), np.arange(1, n, 2)])
    turns = (np.arange(n)[:, None] * (2 * k[None, :] + 1)) % (4 * n)
    angle = turns * (math.pi / (2 * n))
    table = np.concatenate([np.cos(angle), -np.sin(angle)], axis=1)
    high = table.astype(ml_dtypes.bfloat16)
    low = (table - high.astype(np.float64)).astype(ml_dtypes.bfloat16)
    return high, low


def dot(a, b):
    return jnp.dot(a, b, preferred_element_type=jnp.float32)


def dot_nt(a, b):
    return lax.dot_general(a, b, NT, preferred_element_type=jnp.float32)


def corr(fr, fi, gr, gi):
    return fr * gr + fi * gi, fr * gi - fi * gr


def kernel(
    n_ctx, n_dp,
    g_hbm, x_hbm, f_hbm, wh_hbm, wl_hbm,
    dx_ref, h_ref,
    g_in, x_in, f_in, wh, wl,
    out1, outf, in1, inf, spec, specf, s_hi, s_lo, h_out, dx_out, h_in, dx_in,
    load_sem, send1, recv1, sendf, recvf, send_h, recv_h, send_dx, recv_dx,
):
    n, width = g_hbm.shape
    group = n_ctx * n_dp
    cb = width // group
    half_lanes = n // 2
    ctx = lax.axis_index("context")
    dp = lax.axis_index("dp")
    me = ctx * n_dp + dp

    barrier = pltpu.get_barrier_semaphore()
    offsets = [(dc, dd) for dc in range(n_ctx - 1, -1, -1) for dd in range(n_dp - 1, -1, -1)]
    remote = [o for o in offsets if o != (0, 0)]

    def ahead(dc, dd):
        return lax.rem(ctx + dc, n_ctx), lax.rem(dp + dd, n_dp)

    def behind(dc, dd):
        return lax.rem(ctx + n_ctx - dc, n_ctx), lax.rem(dp + n_dp - dd, n_dp)

    for o in remote:
        pc, pd = ahead(*o)
        pl.semaphore_signal(barrier, inc=1, device_id={"context": pc, "dp": pd}, device_id_type=MESH)
    loads = [
        pltpu.make_async_copy(src, dst, load_sem.at[i])
        for i, (src, dst) in enumerate(
            [(g_hbm, g_in), (x_hbm, x_in), (f_hbm, f_in), (wh_hbm, wh), (wl_hbm, wl)]
        )
    ]
    for c in loads:
        c.start()
    loads[0].wait()
    out1[:, 0] = g_in[...].T.reshape(group, cb, n)
    loads[1].wait()
    out1[:, 1] = x_in[...].T.reshape(group, cb, n)
    loads[2].wait()
    outf[...] = f_in[...].T.reshape(group, cb, n)
    pl.semaphore_wait(barrier, group - 1)

    def to_peer(o):
        pc, pd = ahead(*o)
        peer = pc * n_dp + pd
        return pltpu.make_async_remote_copy(
            src_ref=out1.at[peer], dst_ref=in1.at[ctx, dp],
            send_sem=send1.at[peer], recv_sem=recv1.at[me],
            device_id={"context": pc, "dp": pd}, device_id_type=MESH,
        )

    sent = [to_peer(o) for o in remote]
    for c in sent:
        c.start()
    for dc in range(1, n_ctx):
        pc, _ = ahead(dc, 0)
        c = pltpu.make_async_remote_copy(
            src_ref=outf.at[pc * n_dp + dp], dst_ref=inf.at[ctx],
            send_sem=sendf.at[dc], recv_sem=recvf.at[ctx],
            device_id={"context": pc, "dp": dp}, device_id_type=MESH,
        )
        c.start()
        sent.append(c)
    in1[ctx, dp] = out1[me]
    inf[ctx] = outf[me]
    loads[3].wait()
    loads[4].wait()
    for o in remote:
        sc, sd = behind(*o)
        pltpu.make_async_remote_copy(
            src_ref=out1.at[me], dst_ref=in1.at[sc, sd],
            send_sem=send1.at[me], recv_sem=recv1.at[sc * n_dp + sd],
            device_id={"context": sc, "dp": sd}, device_id_type=MESH,
        ).wait_recv()
    for dc in range(1, n_ctx):
        sc, _ = behind(dc, 0)
        pltpu.make_async_remote_copy(
            src_ref=outf.at[me], dst_ref=inf.at[sc],
            send_sem=sendf.at[0], recv_sem=recvf.at[sc],
            device_id={"context": sc, "dp": dp}, device_id_type=MESH,
        ).wait_recv()

    rows = in1[...].reshape(group * 2 * cb, n)
    spec[...] = (dot(rows, wh[...]) + dot(rows, wl[...])).reshape(spec.shape)
    rows_f = inf[...].reshape(n_ctx * cb, n)
    specf[...] = (dot(rows_f, wh[...]) + dot(rows_f, wl[...])).reshape(specf.shape)

    def put(row, lanes, value):
        high = value.astype(jnp.bfloat16)
        s_hi[pl.ds(row, cb), lanes] = high
        s_lo[pl.ds(row, cb), lanes] = (value - high.astype(jnp.float32)).astype(jnp.bfloat16)

    for parity in range(2):
        re = pl.ds(parity * half_lanes, half_lanes)
        im = pl.ds(n + parity * half_lanes, half_lanes)
        f0r, f0i = specf[0, :, re], specf[0, :, im]
        f1r, f1i = specf[1, :, re], specf[1, :, im]
        h0r = h0i = h1r = h1i = jnp.zeros((cb, half_lanes), jnp.float32)
        for b in range(n_dp):
            g0r, g0i = spec[0, b, 0, :, re], spec[0, b, 0, :, im]
            g1r, g1i = spec[1, b, 0, :, re], spec[1, b, 0, :, im]
            x0r, x0i = spec[0, b, 1, :, re], spec[0, b, 1, :, im]
            x1r, x1i = spec[1, b, 1, :, re], spec[1, b, 1, :, im]
            if parity == 0:
                qr, qi = g0r + g1i, g0i - g1r
            else:
                qr, qi = g0r - g1i, g0i + g1r
            ar, ai = corr(x0r, x0i, qr, qi)
            br, bi = corr(x1r, x1i, g1r, g1i)
            cr, ci = corr(x0r, x0i, g1r, g1i)
            h0r, h0i = h0r + (ar + br), h0i + (ai + bi)
            h1r, h1i = h1r + cr, h1i + ci
            ar, ai = corr(f0r, f0i, qr, qi)
            br, bi = corr(f1r, f1i, g1r, g1i)
            cr, ci = corr(f0r, f0i, g1r, g1i)
            row = n_ctx * cb + b * cb
            put(row, re, ar + br)
            put(row, im, ai + bi)
            put(row + n_dp * cb, re, cr)
            put(row + n_dp * cb, im, ci)
        put(0, re, h0r)
        put(0, im, h0i)
        put(cb, re, h1r)
        put(cb, im, h1i)

    def inverse(start, size):
        high, low = s_hi[pl.ds(start, size), :], s_lo[pl.ds(start, size), :]
        total = dot_nt(high, wh[...]) + (dot_nt(low, wh[...]) + dot_nt(high, wl[...]))
        return total * (1.0 / n)

    h_out[...] = inverse(0, n_ctx * cb).reshape(h_out.shape)
    for o in remote:
        pc, pd = ahead(*o)
        peer = pc * n_dp + pd
        c = pltpu.make_async_remote_copy(
            src_ref=h_out.at[pc], dst_ref=h_in.at[me],
            send_sem=send_h.at[peer], recv_sem=recv_h.at[me],
            device_id={"context": pc, "dp": pd}, device_id_type=MESH,
        )
        c.start()
        sent.append(c)
    dx_out[...] = inverse(n_ctx * cb, group * cb).astype(jnp.bfloat16).reshape(dx_out.shape)
    for o in remote:
        pc, pd = ahead(*o)
        peer = pc * n_dp + pd
        c = pltpu.make_async_remote_copy(
            src_ref=dx_out.at[pc, pd], dst_ref=dx_in.at[me],
            send_sem=send_dx.at[peer], recv_sem=recv_dx.at[me],
            device_id={"context": pc, "dp": pd}, device_id_type=MESH,
        )
        c.start()
        sent.append(c)
    h_in[me] = h_out[ctx]
    dx_in[me] = dx_out[ctx, dp]
    for o in remote:
        sc, sd = behind(*o)
        source = sc * n_dp + sd
        pltpu.make_async_remote_copy(
            src_ref=h_out.at[0], dst_ref=h_in.at[source],
            send_sem=send_h.at[me], recv_sem=recv_h.at[source],
            device_id={"context": sc, "dp": sd}, device_id_type=MESH,
        ).wait_recv()
    h_ref[...] = h_in[...].reshape(width, n).T
    for o in remote:
        sc, sd = behind(*o)
        source = sc * n_dp + sd
        pltpu.make_async_remote_copy(
            src_ref=dx_out.at[0, 0], dst_ref=dx_in.at[source],
            send_sem=send_dx.at[me], recv_sem=recv_dx.at[source],
            device_id={"context": sc, "dp": sd}, device_id_type=MESH,
        ).wait_recv()
    dx_ref[...] = dx_in[...].reshape(width, n).T
    for c in sent:
        c.wait_send()


def fused_body(n_ctx, n_dp, grad_out, inputs, filt):
    n, width = filt.shape
    group = n_ctx * n_dp
    cb = width // group
    high, low = half_step_table(n)
    bf16, f32 = jnp.bfloat16, jnp.float32
    sems = pltpu.SemaphoreType.DMA
    any_spec = pl.BlockSpec(memory_space=pl.ANY)
    vmem_spec = pl.BlockSpec(memory_space=pltpu.VMEM)
    dx, h = pl.pallas_call(
        functools.partial(kernel, n_ctx, n_dp),
        out_shape=(
            jax.ShapeDtypeStruct((n, width), bf16),
            jax.ShapeDtypeStruct((n, width), f32),
        ),
        in_specs=[any_spec] * 5,
        out_specs=(vmem_spec, vmem_spec),
        scratch_shapes=[
            pltpu.VMEM((n, width), bf16),
            pltpu.VMEM((n, width), bf16),
            pltpu.VMEM((n, width), bf16),
            pltpu.VMEM((n, 2 * n), bf16),
            pltpu.VMEM((n, 2 * n), bf16),
            pltpu.VMEM((group, 2, cb, n), bf16),
            pltpu.VMEM((group, cb, n), bf16),
            pltpu.VMEM((n_ctx, n_dp, 2, cb, n), bf16),
            pltpu.VMEM((n_ctx, cb, n), bf16),
            pltpu.VMEM((n_ctx, n_dp, 2, cb, 2 * n), f32),
            pltpu.VMEM((n_ctx, cb, 2 * n), f32),
            pltpu.VMEM((n_ctx * cb + group * cb, 2 * n), bf16),
            pltpu.VMEM((n_ctx * cb + group * cb, 2 * n), bf16),
            pltpu.VMEM((n_ctx, cb, n), f32),
            pltpu.VMEM((n_ctx, n_dp, cb, n), bf16),
            pltpu.VMEM((group, cb, n), f32),
            pltpu.VMEM((group, cb, n), bf16),
            sems((5,)),
            sems((group,)), sems((group,)),
            sems((n_ctx,)), sems((n_ctx,)),
            sems((group,)), sems((group,)),
            sems((group,)), sems((group,)),
        ],
        compiler_params=pltpu.CompilerParams(
            collective_id=0, has_side_effects=True, vmem_limit_bytes=40 * 1024 * 1024
        ),
    )(
        grad_out.reshape(n, width), inputs.reshape(n, width), filt,
        jnp.asarray(high), jnp.asarray(low),
    )
    return dx.reshape(grad_out.shape), h


full_turn = 2.0 * math.pi


def rotation(left_idx, right_idx, modulus):
    angle = (left_idx * right_idx % modulus).astype(jnp.float32) * (full_turn / modulus)
    return (jnp.cos(angle), jnp.sin(angle))


def contract(form, table, values):
    return jnp.einsum(
        form, table, values, precision=lax.Precision.HIGHEST, preferred_element_type=jnp.float32
    )


def first_section(part, cos_first, sin_first, cos_twist, sin_twist, members, piece_rows):
    values = part.astype(jnp.float32)
    values = values.reshape(values.shape[0], members, piece_rows, values.shape[2])
    real_part = contract("fn,knbc->kfbc", cos_first, values)
    imag_part = -contract("fn,knbc->kfbc", sin_first, values)
    cos_wide = cos_twist[None, :, :, None]
    sin_wide = sin_twist[None, :, :, None]
    return jnp.stack(
        [real_part * cos_wide + imag_part * sin_wide, imag_part * cos_wide - real_part * sin_wide]
    )


def second_section(mixed, cos_second, sin_second):
    real_in = mixed[0]
    imag_in = mixed[1]
    real_out = contract("fn,kgnc->kgfc", cos_second, real_in) + contract(
        "fn,kgnc->kgfc", sin_second, imag_in
    )
    imag_out = contract("fn,kgnc->kgfc", cos_second, imag_in) - contract(
        "fn,kgnc->kgfc", sin_second, real_in
    )
    return (real_out, imag_out)


def body(grad_out, inputs, filt):
    members = lax.axis_size("context")
    position = lax.axis_index("context")
    seq_rows = grad_out.shape[1]
    piece_rows = seq_rows // members
    spread = 2 * members
    modulus = spread * seq_rows
    freq_first = jnp.arange(spread, dtype=jnp.int32)
    dev_first = jnp.arange(members, dtype=jnp.int32)
    cos_first, sin_first = rotation(freq_first[:, None], dev_first[None, :], spread)
    local_rows = position * piece_rows + jnp.arange(piece_rows, dtype=jnp.int32)
    cos_twist, sin_twist = rotation(freq_first[:, None], local_rows[None, :], modulus)
    all_rows = jnp.arange(seq_rows, dtype=jnp.int32)
    cos_second, sin_second = rotation(all_rows[:, None], all_rows[None, :], seq_rows)
    signals = jnp.concatenate([grad_out, inputs], axis=0)
    replicas = lax.axis_size("dp")
    width = filt.shape[1] // replicas
    own_filter = lax.dynamic_slice_in_dim(filt, lax.axis_index("dp") * width, width, 1)[None]
    column_sig, column_filt = (
        lax.all_to_all(signals, "context", split_axis=1, concat_axis=1, tiled=True),
        lax.all_to_all(own_filter, "context", split_axis=1, concat_axis=1, tiled=True),
    )
    sectioned_sig = first_section(
        column_sig, cos_first, sin_first, cos_twist, sin_twist, members, piece_rows
    )
    sectioned_filt = first_section(
        column_filt, cos_first, sin_first, cos_twist, sin_twist, members, piece_rows
    )
    mixed_sig, mixed_filt = (
        lax.all_to_all(sectioned_sig, "context", split_axis=2, concat_axis=3, tiled=True),
        lax.all_to_all(sectioned_filt, "context", split_axis=2, concat_axis=3, tiled=True),
    )
    sig_re, sig_im = second_section(mixed_sig, cos_second, sin_second)
    filt_re, filt_im = second_section(mixed_filt, cos_second, sin_second)
    filt_re, filt_im = (
        lax.all_gather(filt_re, "dp", axis=3, tiled=True),
        lax.all_gather(filt_im, "dp", axis=3, tiled=True),
    )
    grad_re = sig_re[0]
    grad_im = sig_im[0]
    input_re = sig_re[1]
    input_im = sig_im[1]
    kernel_re = filt_re[0]
    kernel_im = filt_im[0]
    dx_re = grad_re * kernel_re + grad_im * kernel_im
    dx_im = grad_im * kernel_re - grad_re * kernel_im
    dh_re = grad_re * input_re + grad_im * input_im
    dh_im = grad_im * input_re - grad_re * input_im
    spec_re = jnp.stack([dx_re, dh_re])
    spec_im = jnp.stack([dx_im, dh_im])
    back_re = contract("nf,sgfc->sgnc", cos_second, spec_re) - contract(
        "nf,sgfc->sgnc", sin_second, spec_im
    )
    back_im = contract("nf,sgfc->sgnc", cos_second, spec_im) + contract(
        "nf,sgfc->sgnc", sin_second, spec_re
    )
    own_freq = 2 * position + jnp.arange(2, dtype=jnp.int32)
    cos_back, sin_back = rotation(own_freq[:, None], all_rows[None, :], modulus)
    cos_wide = cos_back[None, :, :, None]
    sin_wide = sin_back[None, :, :, None]
    turned = jnp.stack(
        [back_re * cos_wide - back_im * sin_wide, back_im * cos_wide + back_re * sin_wide]
    )
    regrouped = lax.all_to_all(turned, "context", split_axis=3, concat_axis=2, tiled=True)
    in_time = contract("fn,sfbc->snbc", cos_first, regrouped[0]) - contract(
        "fn,sfbc->snbc", sin_first, regrouped[1]
    )
    in_time = in_time * (1.0 / modulus)
    restored = lax.all_to_all(in_time, "context", split_axis=1, concat_axis=2, tiled=True)
    input_grad = restored[0].astype(jnp.bfloat16)
    filter_grad = lax.psum(restored[1, 0], "dp")
    return (input_grad, filter_grad)


def any_body(n_ctx, n_dp, grad_out, inputs, filt):
    n, width = filt.shape
    tile = 32
    fits = (
        n_ctx == 2
        and grad_out.shape[0] == 1
        and n % 256 == 0
        and width % (n_ctx * n_dp * tile) == 0
        and 16 * n * (n + width) * 4 <= 40 * 1024 * 1024
    )
    if fits:
        return fused_body(n_ctx, n_dp, grad_out, inputs, filt)
    return body(grad_out, inputs, filt)


def solution(mesh):
    return jax.shard_map(
        functools.partial(any_body, mesh.shape["context"], mesh.shape["dp"]),
        mesh=mesh,
        in_specs=(
            P("dp", "context", "tensor"),
            P("dp", "context", "tensor"),
            P("context", "tensor"),
        ),
        out_specs=(P("dp", "context", "tensor"), P("context", "tensor")),
        check_vma=False,
    )
```

profile of v0, /device:TPU:0, one launch (start us, length us, event | category | flops | bytes accessed | tf_op | source)
XLA Modules:
  0.0 22.8 jit_solution(6553379885596713447)
XLA Ops:
  0.6 0.0 copy-start
  0.6 0.9 %copy-done = bf16[256,512]{1,0:T(8,128)(2,1)S(1)} copy-done((bf16[256,512]{1,0:T(8,128)(2,1)S(1)}, bf16[256,512]{1,0:T(8,128)(2,1)}, u32[]{:S(2)}) %copy-start) | copy-done | bytes 262168
  1.6 0.0 copy-start.1
  1.6 0.9 %copy-done.1 = bf16[256,512]{1,0:T(8,128)(2,1)S(1)} copy-done((bf16[256,512]{1,0:T(8,128)(2,1)S(1)}, bf16[256,512]{1,0:T(8,128)(2,1)}, u32[]{:S(2)}) %copy-start.1) | copy-done | bytes 262168
  2.5 0.0 copy-start.2
  2.5 0.9 %copy-done.2 = bf16[1,256,256]{2,1,0:T(8,128)(2,1)S(1)} copy-done((bf16[1,256,256]{2,1,0:T(8,128)(2,1)S(1)}, bf16[1,256,256]{2,1,0:T(8,128)(2,1)}, u32[]{:S(2)}) %copy-start.2) | copy-done | bytes 131096
  3.4 0.0 copy-start.3
  3.4 0.9 %copy-done.3 = bf16[1,256,256]{2,1,0:T(8,128)(2,1)S(1)} copy-done((bf16[1,256,256]{2,1,0:T(8,128)(2,1)S(1)}, bf16[1,256,256]{2,1,0:T(8,128)(2,1)}, u32[]{:S(2)}) %copy-start.3) | copy-done | bytes 131096
  4.3 0.0 copy-start.4
  4.3 0.9 %copy-done.4 = bf16[256,256]{1,0:T(8,128)(2,1)S(1)} copy-done((bf16[256,256]{1,0:T(8,128)(2,1)S(1)}, bf16[256,256]{1,0:T(8,128)(2,1)}, u32[]{:S(2)}) %copy-start.4) | copy-done | bytes 131096
  5.2 16.2 %shard_map.68 = (bf16[256,256]{1,0:T(8,128)(2,1)S(1)}, f32[256,256]{1,0:T(8,128)S(1)}) custom-call(bf16[256,256]{1,0:T(8,128)(2,1)S(1)} %bitcast.3, bf16[256,256]{1,0:T(8,128)(2,1)S(1)} %bitcast.4, bf16[256,256]{1,0:T(8,128)(2,1)S(1)} %copy-done.4, bf16[256,512]{1,0:T(8,128)(2,1)S(1)} %copy-done.1, bf16[256,512]{1,0:T(8,128)(2,1)S(1)} %copy-done), custom_call_target="tpu_custom_call" | custom-call | tf_op jit(solution)/shard_map/pallas_call | solution.py:227
  21.4 0.7 %copy.9 = bf16[1,256,256]{2,1,0:T(8,128)(2,1)} copy(bf16[1,256,256]{2,1,0:T(8,128)(2,1)S(1)} %bitcast.5) | data formatting | bytes 262144
  22.1 0.7 %copy.10 = f32[256,256]{1,0:T(8,128)} copy(f32[256,256]{1,0:T(8,128)S(1)} %get-tuple-element.9) | data formatting | bytes 524288
Async XLA Ops:
  0.6 1.0 %copy-start = (bf16[256,512]{1,0:T(8,128)(2,1)S(1)}, bf16[256,512]{1,0:T(8,128)(2,1)}, u32[]{:S(2)}) copy-start(bf16[256,512]{1,0:T(8,128)(2,1)} %constant.5.clone.wl_hbm) | copy-start | bytes 786436
  1.6 0.9 %copy-start.1 = (bf16[256,512]{1,0:T(8,128)(2,1)S(1)}, bf16[256,512]{1,0:T(8,128)(2,1)}, u32[]{:S(2)}) copy-start(bf16[256,512]{1,0:T(8,128)(2,1)} %constant.4.clone.wh_hbm) | copy-start | bytes 786436
  2.5 0.9 %copy-start.2 = (bf16[1,256,256]{2,1,0:T(8,128)(2,1)S(1)}, bf16[1,256,256]{2,1,0:T(8,128)(2,1)}, u32[]{:S(2)}) copy-start(bf16[1,256,256]{2,1,0:T(8,128)(2,1)} %param.5) | copy-start | bytes 393220
  3.4 0.9 %copy-start.3 = (bf16[1,256,256]{2,1,0:T(8,128)(2,1)S(1)}, bf16[1,256,256]{2,1,0:T(8,128)(2,1)}, u32[]{:S(2)}) copy-start(bf16[1,256,256]{2,1,0:T(8,128)(2,1)} %param.6) | copy-start | bytes 393220
  4.3 0.9 %copy-start.4 = (bf16[256,256]{1,0:T(8,128)(2,1)S(1)}, bf16[256,256]{1,0:T(8,128)(2,1)}, u32[]{:S(2)}) copy-start(bf16[256,256]{1,0:T(8,128)(2,1)} %f_hbm.1) | copy-start | bytes 393220
where the time goes:
time: 23 us; the launch traced here: 22.8 us
  Pallas kernels  16.2 us (70%)
  local copies, waits for them, and re-layouts  5.97 us (26%)
  between operations  0.65 us (3%)
    pallas_call x1, Pallas kernels, fused_body(): pl.pallas_call(functools.partial(kernel, n_ctx, n_dp), out_shape=(jax.Sha...  16.2 us
    unnamed x12, local copies, waits for them, and re-layouts  5.97 us

commit v1 on v0

--- a/solution.py
+++ b/solution.py
@@ -42,7 +42,7 @@
     dx_ref, h_ref,
     g_in, x_in, f_in, wh, wl,
     out1, outf, in1, inf, spec, specf, s_hi, s_lo, h_out, dx_out, h_in, dx_in,
-    load_sem, send1, recv1, sendf, recvf, send_h, recv_h, send_dx, recv_dx,
+    load_sem, send1, recv1, sendf, recvf, send_h, recv_h, send_f, send_dx, recv_dx,
 ):
     n, width = g_hbm.shape
     group = n_ctx * n_dp
@@ -73,144 +73,164 @@
     ]
     for c in loads:
         c.start()
-    loads[0].wait()
-    out1[:, 0] = g_in[...].T.reshape(group, cb, n)
-    loads[1].wait()
-    out1[:, 1] = x_in[...].T.reshape(group, cb, n)
-    loads[2].wait()
-    outf[...] = f_in[...].T.reshape(group, cb, n)
-    pl.semaphore_wait(barrier, group - 1)
-
-    def to_peer(o):
-        pc, pd = ahead(*o)
-        peer = pc * n_dp + pd
-        return pltpu.make_async_remote_copy(
-            src_ref=out1.at[peer], dst_ref=in1.at[ctx, dp],
-            send_sem=send1.at[peer], recv_sem=recv1.at[me],
+
+    sib = dp + 1 - 2 * lax.rem(dp, 2)
+    sent = []
+
+    def push(src, dst, send, recv, pc, pd):
+        c = pltpu.make_async_remote_copy(
+            src_ref=src, dst_ref=dst, send_sem=send, recv_sem=recv,
             device_id={"context": pc, "dp": pd}, device_id_type=MESH,
-        )
-
-    sent = [to_peer(o) for o in remote]
-    for c in sent:
-        c.start()
-    for dc in range(1, n_ctx):
-        pc, _ = ahead(dc, 0)
-        c = pltpu.make_async_remote_copy(
-            src_ref=outf.at[pc * n_dp + dp], dst_ref=inf.at[ctx],
-            send_sem=sendf.at[dc], recv_sem=recvf.at[ctx],
-            device_id={"context": pc, "dp": dp}, device_id_type=MESH,
         )
         c.start()
         sent.append(c)
+
+    def arrived(src, dst, send, recv, pc, pd):
+        pltpu.make_async_remote_copy(
+            src_ref=src, dst_ref=dst, send_sem=send, recv_sem=recv,
+            device_id={"context": pc, "dp": pd}, device_id_type=MESH,
+        ).wait_recv()
+
+    part = n_dp * cb
+
+    def turn(src, c):
+        lanes = pl.ds(pl.multiple_of(c * part, part), part)
+        return src[:, lanes].T.reshape(n_dp, cb, n)
+
+    for i, src in enumerate((g_in, x_in)):
+        loads[i].wait()
+    for dc in range(n_ctx - 1, -1, -1):
+        pc, _ = ahead(dc, 0)
+        blocks = pl.ds(pc * n_dp, n_dp)
+        out1[blocks, 0] = turn(g_in, pc)
+        out1[blocks, 1] = turn(x_in, pc)
+        if dc == n_ctx - 1:
+            pl.semaphore_wait(barrier, group - 1)
+        for dd in range(n_dp - 1, -1, -1):
+            if (dc, dd) != (0, 0):
+                _, pd = ahead(dc, dd)
+                peer = pc * n_dp + pd
+                push(out1.at[peer], in1.at[ctx, dp], send1.at[peer], recv1.at[me], pc, pd)
+    loads[2].wait()
+    outf[...] = f_in[...].T.reshape(group, cb, n)
+    for dc in range(1, n_ctx):
+        pc, _ = ahead(dc, 0)
+        push(outf.at[pc * n_dp + dp], inf.at[ctx], sendf.at[dc], recvf.at[ctx], pc, dp)
     in1[ctx, dp] = out1[me]
     inf[ctx] = outf[me]
     loads[3].wait()
     loads[4].wait()
-    for o in remote:
-        sc, sd = behind(*o)
-        pltpu.make_async_remote_copy(
-            src_ref=out1.at[me], dst_ref=in1.at[sc, sd],
-            send_sem=send1.at[me], recv_sem=recv1.at[sc * n_dp + sd],
-            device_id={"context": sc, "dp": sd}, device_id_type=MESH,
-        ).wait_recv()
-    for dc in range(1, n_ctx):
+
+    for dc in range(n_ctx):
         sc, _ = behind(dc, 0)
-        pltpu.make_async_remote_copy(
-            src_ref=outf.at[me], dst_ref=inf.at[sc],
-            send_sem=sendf.at[0], recv_sem=recvf.at[sc],
-            device_id={"context": sc, "dp": dp}, device_id_type=MESH,
-        ).wait_recv()
-
-    rows = in1[...].reshape(group * 2 * cb, n)
-    spec[...] = (dot(rows, wh[...]) + dot(rows, wl[...])).reshape(spec.shape)
-    rows_f = inf[...].reshape(n_ctx * cb, n)
-    specf[...] = (dot(rows_f, wh[...]) + dot(rows_f, wl[...])).reshape(specf.shape)
+        for dd in range(n_dp):
+            if (dc, dd) != (0, 0):
+                _, sd = behind(dc, dd)
+                arrived(out1.at[me], in1.at[sc, sd], send1.at[me], recv1.at[sc * n_dp + sd], sc, sd)
+        rows = in1[sc].reshape(n_dp * 2 * cb, n)
+        spec[sc] = (dot(rows, wh[...]) + dot(rows, wl[...])).reshape(n_dp, 2, cb, 2 * n)
 
     def put(row, lanes, value):
         high = value.astype(jnp.bfloat16)
         s_hi[pl.ds(row, cb), lanes] = high
         s_lo[pl.ds(row, cb), lanes] = (value - high.astype(jnp.float32)).astype(jnp.bfloat16)
 
+    def shifted(parity, b, re, im):
+        g0r, g0i = spec[0, b, 0, :, re], spec[0, b, 0, :, im]
+        g1r, g1i = spec[1, b, 0, :, re], spec[1, b, 0, :, im]
+        if parity == 0:
+            return g0r + g1i, g0i - g1r, g1r, g1i
+        return g0r - g1i, g0i + g1r, g1r, g1i
+
+    def lanes_of(parity):
+        return pl.ds(parity * half_lanes, half_lanes), pl.ds(n + parity * half_lanes, half_lanes)
+
+    def inverse(start, size):
+        rows = pl.ds(start, size)
+        high, low = s_hi[rows, :], s_lo[rows, :]
+        total = dot_nt(high, wh[...]) + (dot_nt(low, wh[...]) + dot_nt(high, wl[...]))
+        return total * (1.0 / n)
+
     for parity in range(2):
-        re = pl.ds(parity * half_lanes, half_lanes)
-        im = pl.ds(n + parity * half_lanes, half_lanes)
-        f0r, f0i = specf[0, :, re], specf[0, :, im]
-        f1r, f1i = specf[1, :, re], specf[1, :, im]
+        re, im = lanes_of(parity)
         h0r = h0i = h1r = h1i = jnp.zeros((cb, half_lanes), jnp.float32)
         for b in range(n_dp):
-            g0r, g0i = spec[0, b, 0, :, re], spec[0, b, 0, :, im]
-            g1r, g1i = spec[1, b, 0, :, re], spec[1, b, 0, :, im]
+            qr, qi, g1r, g1i = shifted(parity, b, re, im)
             x0r, x0i = spec[0, b, 1, :, re], spec[0, b, 1, :, im]
             x1r, x1i = spec[1, b, 1, :, re], spec[1, b, 1, :, im]
-            if parity == 0:
-                qr, qi = g0r + g1i, g0i - g1r
-            else:
-                qr, qi = g0r - g1i, g0i + g1r
             ar, ai = corr(x0r, x0i, qr, qi)
             br, bi = corr(x1r, x1i, g1r, g1i)
             cr, ci = corr(x0r, x0i, g1r, g1i)
             h0r, h0i = h0r + (ar + br), h0i + (ai + bi)
             h1r, h1i = h1r + cr, h1i + ci
-            ar, ai = corr(f0r, f0i, qr, qi)
-            br, bi = corr(f1r, f1i, g1r, g1i)
-            cr, ci = corr(f0r, f0i, g1r, g1i)
-            row = n_ctx * cb + b * cb
-            put(row, re, ar + br)
-            put(row, im, ai + bi)
-            put(row + n_dp * cb, re, cr)
-            put(row + n_dp * cb, im, ci)
         put(0, re, h0r)
         put(0, im, h0i)
         put(cb, re, h1r)
         put(cb, im, h1i)
-
-    def inverse(start, size):
-        high, low = s_hi[pl.ds(start, size), :], s_lo[pl.ds(start, size), :]
-        total = dot_nt(high, wh[...]) + (dot_nt(low, wh[...]) + dot_nt(high, wl[...]))
-        return total * (1.0 / n)
-
     h_out[...] = inverse(0, n_ctx * cb).reshape(h_out.shape)
-    for o in remote:
-        pc, pd = ahead(*o)
-        peer = pc * n_dp + pd
-        c = pltpu.make_async_remote_copy(
-            src_ref=h_out.at[pc], dst_ref=h_in.at[me],
-            send_sem=send_h.at[peer], recv_sem=recv_h.at[me],
-            device_id={"context": pc, "dp": pd}, device_id_type=MESH,
-        )
-        c.start()
-        sent.append(c)
-    dx_out[...] = inverse(n_ctx * cb, group * cb).astype(jnp.bfloat16).reshape(dx_out.shape)
-    for o in remote:
-        pc, pd = ahead(*o)
-        peer = pc * n_dp + pd
-        c = pltpu.make_async_remote_copy(
-            src_ref=dx_out.at[pc, pd], dst_ref=dx_in.at[me],
-            send_sem=send_dx.at[peer], recv_sem=recv_dx.at[me],
-            device_id={"context": pc, "dp": pd}, device_id_type=MESH,
-        )
-        c.start()
-        sent.append(c)
+    for dc, dd in remote:
+        if dd % 2 == 0:
+            pc, pd = ahead(dc, dd)
+            push(h_out.at[pc], h_in.at[me], send_h.at[pc * n_dp + pd], recv_h.at[me], pc, pd)
+    push(h_out.at[ctx], h_in.at[me], send_h.at[ctx * n_dp + sib], recv_h.at[me], ctx, sib)
     h_in[me] = h_out[ctx]
+
+    for dc in range(1, n_ctx):
+        sc, _ = behind(dc, 0)
+        arrived(outf.at[me], inf.at[sc], sendf.at[0], recvf.at[sc], sc, dp)
+    rows_f = inf[...].reshape(n_ctx * cb, n)
+    specf[...] = (dot(rows_f, wh[...]) + dot(rows_f, wl[...])).reshape(specf.shape)
+    first = n_ctx * cb
+    for parity in range(2):
+        re, im = lanes_of(parity)
+        f0r, f0i = specf[0, :, re], specf[0, :, im]
+        f1r, f1i = specf[1, :, re], specf[1, :, im]
+        for b in range(n_dp):
+            qr, qi, g1r, g1i = shifted(parity, b, re, im)
+            ar, ai = corr(f0r, f0i, qr, qi)
+            br, bi = corr(f1r, f1i, g1r, g1i)
+            cr, ci = corr(f0r, f0i, g1r, g1i)
+            row = first + b * cb
+            put(row, re, ar + br)
+            put(row, im, ai + bi)
+            put(row + part, re, cr)
+            put(row + part, im, ci)
+    for dc in range(n_ctx - 1, -1, -1):
+        pc, _ = ahead(dc, 0)
+        start = pl.multiple_of(first + pc * part, cb)
+        dx_out[pc] = inverse(start, part).astype(jnp.bfloat16).reshape(n_dp, cb, n)
+        for dd in range(n_dp - 1, -1, -1):
+            if (dc, dd) != (0, 0):
+                _, pd = ahead(dc, dd)
+                push(dx_out.at[pc, pd], dx_in.at[me], send_dx.at[pc * n_dp + pd], recv_dx.at[me], pc, pd)
     dx_in[me] = dx_out[ctx, dp]
-    for o in remote:
-        sc, sd = behind(*o)
+
+    def h_arrived(sc, sd):
         source = sc * n_dp + sd
-        pltpu.make_async_remote_copy(
-            src_ref=h_out.at[0], dst_ref=h_in.at[source],
-            send_sem=send_h.at[me], recv_sem=recv_h.at[source],
-            device_id={"context": sc, "dp": sd}, device_id_type=MESH,
-        ).wait_recv()
-    h_ref[...] = h_in[...].reshape(width, n).T
-    for o in remote:
-        sc, sd = behind(*o)
-        source = sc * n_dp + sd
-        pltpu.make_async_remote_copy(
-            src_ref=dx_out.at[0, 0], dst_ref=dx_in.at[source],
-            send_sem=send_dx.at[me], recv_sem=recv_dx.at[source],
-            device_id={"context": sc, "dp": sd}, device_id_type=MESH,
-        ).wait_recv()
-    dx_ref[...] = dx_in[...].reshape(width, n).T
+        arrived(h_out.at[0], h_in.at[source], send_h.at[me], recv_h.at[source], sc, sd)
+        return source
+
+    def finish(sc, src, dst):
+        lanes = pl.ds(pl.multiple_of(sc * part, part), part)
+        dst[:, lanes] = src[pl.ds(sc * n_dp, n_dp)].reshape(part, n).T
+
+    for dc in range(n_ctx):
+        for dd in range(0, n_dp, 2):
+            if (dc, dd) != (0, 0):
+                source = h_arrived(*behind(dc, dd))
+                push(h_in.at[source], h_in.at[source], send_f.at[source], recv_h.at[source], ctx, sib)
+    for dc in range(n_ctx):
+        for dd in range(1, n_dp, 2):
+            h_arrived(*behind(dc, dd))
+        finish(behind(dc, 0)[0], h_in, h_ref)
+    for dc in range(n_ctx):
+        sc, _ = behind(dc, 0)
+        for dd in range(n_dp):
+            if (dc, dd) != (0, 0):
+                _, sd = behind(dc, dd)
+                source = sc * n_dp + sd
+                arrived(dx_out.at[0, 0], dx_in.at[source], send_dx.at[me], recv_dx.at[source], sc, sd)
+        finish(sc, dx_in, dx_ref)
     for c in sent:
         c.wait_send()
 
@@ -222,7 +242,7 @@
     high, low = half_step_table(n)
     bf16, f32 = jnp.bfloat16, jnp.float32
     sems = pltpu.SemaphoreType.DMA
-    any_spec = pl.BlockSpec(memory_space=pl.ANY)
+    hbm_spec = pl.BlockSpec(memory_space=pltpu.HBM)
     vmem_spec = pl.BlockSpec(memory_space=pltpu.VMEM)
     dx, h = pl.pallas_call(
         functools.partial(kernel, n_ctx, n_dp),
@@ -230,7 +250,7 @@
             jax.ShapeDtypeStruct((n, width), bf16),
             jax.ShapeDtypeStruct((n, width), f32),
         ),
-        in_specs=[any_spec] * 5,
+        in_specs=[hbm_spec] * 5,
         out_specs=(vmem_spec, vmem_spec),
         scratch_shapes=[
             pltpu.VMEM((n, width), bf16),
@@ -253,7 +273,7 @@
             sems((5,)),
             sems((group,)), sems((group,)),
             sems((n_ctx,)), sems((n_ctx,)),
-            sems((group,)), sems((group,)),
+            sems((group,)), sems((group,)), sems((group,)),
             sems((group,)), sems((group,)),
         ],
         compiler_params=pltpu.CompilerParams(
@@ -384,8 +404,10 @@
     fits = (
         n_ctx == 2
         and grad_out.shape[0] == 1
+        and n_dp % 2 == 0
         and n % 256 == 0
         and width % (n_ctx * n_dp * tile) == 0
+        and width % (n_ctx * 128) == 0
         and 16 * n * (n + width) * 4 <= 40 * 1024 * 1024
     )
     if fits:

time: 23 us -> 22.8 us (level); the launches traced: 22.8 us -> 22.3 us
  Pallas kernels: 16.2 us -> 15.7 us
    pallas_call x1, Pallas kernels: 16.2 us -> 15.7 us  [fused_body(): pl.pallas_call(functools.partial(kernel, n_ctx, n_dp), out_shape=(jax.Sha...]
where the time goes in v1:
time: 22.8 us; the launch traced here: 22.3 us
  Pallas kernels  15.7 us (69%)
  local copies, waits for them, and re-layouts  5.97 us (26%)
  between operations  0.65 us (3%)
    pallas_call x1, Pallas kernels, fused_body(): pl.pallas_call(functools.partial(kernel, n_ctx, n_dp), out_shape=(jax.Sha...  15.7 us
    unnamed x12, local copies, waits for them, and re-layouts  5.97 us

profile of v1, /device:TPU:0, one launch (start us, length us, event | category | flops | bytes accessed | tf_op | source)
XLA Modules:
  0.0 22.3 jit_solution(17461874238246523446)
XLA Ops:
  0.6 0.0 copy-start
  0.6 0.9 %copy-done = bf16[256,512]{1,0:T(8,128)(2,1)S(1)} copy-done((bf16[256,512]{1,0:T(8,128)(2,1)S(1)}, bf16[256,512]{1,0:T(8,128)(2,1)}, u32[]{:S(2)}) %copy-start) | copy-done | bytes 262168
  1.6 0.0 copy-start.1
  1.6 0.9 %copy-done.1 = bf16[256,512]{1,0:T(8,128)(2,1)S(1)} copy-done((bf16[256,512]{1,0:T(8,128)(2,1)S(1)}, bf16[256,512]{1,0:T(8,128)(2,1)}, u32[]{:S(2)}) %copy-start.1) | copy-done | bytes 262168
  2.5 0.0 copy-start.2
  2.5 0.9 %copy-done.2 = bf16[1,256,256]{2,1,0:T(8,128)(2,1)S(1)} copy-done((bf16[1,256,256]{2,1,0:T(8,128)(2,1)S(1)}, bf16[1,256,256]{2,1,0:T(8,128)(2,1)}, u32[]{:S(2)}) %copy-start.2) | copy-done | bytes 131096
  3.4 0.0 copy-start.3
  3.4 0.9 %copy-done.3 = bf16[1,256,256]{2,1,0:T(8,128)(2,1)S(1)} copy-done((bf16[1,256,256]{2,1,0:T(8,128)(2,1)S(1)}, bf16[1,256,256]{2,1,0:T(8,128)(2,1)}, u32[]{:S(2)}) %copy-start.3) | copy-done | bytes 131096
  4.3 0.0 copy-start.4
  4.3 0.9 %copy-done.4 = bf16[256,256]{1,0:T(8,128)(2,1)S(1)} copy-done((bf16[256,256]{1,0:T(8,128)(2,1)S(1)}, bf16[256,256]{1,0:T(8,128)(2,1)}, u32[]{:S(2)}) %copy-start.4) | copy-done | bytes 131096
  5.2 15.7 %shard_map.68 = (bf16[256,256]{1,0:T(8,128)(2,1)S(1)}, f32[256,256]{1,0:T(8,128)S(1)}) custom-call(bf16[256,256]{1,0:T(8,128)(2,1)S(1)} %bitcast.3, bf16[256,256]{1,0:T(8,128)(2,1)S(1)} %bitcast.4, bf16[256,256]{1,0:T(8,128)(2,1)S(1)} %copy-done.4, bf16[256,512]{1,0:T(8,128)(2,1)S(1)} %copy-done.1, bf16[256,512]{1,0:T(8,128)(2,1)S(1)} %copy-done), custom_call_target="tpu_custom_call" | custom-call | tf_op jit(solution)/shard_map/pallas_call | solution.py:247
  21.0 0.7 %copy.9 = bf16[1,256,256]{2,1,0:T(8,128)(2,1)} copy(bf16[1,256,256]{2,1,0:T(8,128)(2,1)S(1)} %bitcast.5) | data formatting | bytes 262144
  21.6 0.7 %copy.10 = f32[256,256]{1,0:T(8,128)} copy(f32[256,256]{1,0:T(8,128)S(1)} %get-tuple-element.9) | data formatting | bytes 524288
Async XLA Ops:
  0.6 1.0 %copy-start = (bf16[256,512]{1,0:T(8,128)(2,1)S(1)}, bf16[256,512]{1,0:T(8,128)(2,1)}, u32[]{:S(2)}) copy-start(bf16[256,512]{1,0:T(8,128)(2,1)} %constant.5.clone.wl_hbm) | copy-start | bytes 786436
  1.6 0.9 %copy-start.1 = (bf16[256,512]{1,0:T(8,128)(2,1)S(1)}, bf16[256,512]{1,0:T(8,128)(2,1)}, u32[]{:S(2)}) copy-start(bf16[256,512]{1,0:T(8,128)(2,1)} %constant.4.clone.wh_hbm) | copy-start | bytes 786436
  2.5 0.9 %copy-start.2 = (bf16[1,256,256]{2,1,0:T(8,128)(2,1)S(1)}, bf16[1,256,256]{2,1,0:T(8,128)(2,1)}, u32[]{:S(2)}) copy-start(bf16[1,256,256]{2,1,0:T(8,128)(2,1)} %param.5) | copy-start | bytes 393220
  3.4 0.9 %copy-start.3 = (bf16[1,256,256]{2,1,0:T(8,128)(2,1)S(1)}, bf16[1,256,256]{2,1,0:T(8,128)(2,1)}, u32[]{:S(2)}) copy-start(bf16[1,256,256]{2,1,0:T(8,128)(2,1)} %param.6) | copy-start | bytes 393220
  4.3 0.9 %copy-start.4 = (bf16[256,256]{1,0:T(8,128)(2,1)S(1)}, bf16[256,256]{1,0:T(8,128)(2,1)}, u32[]{:S(2)}) copy-start(bf16[256,256]{1,0:T(8,128)(2,1)} %f_hbm.1) | copy-start | bytes 393220

commit v2 on v1

--- a/solution.py
+++ b/solution.py
@@ -279,10 +279,13 @@
         compiler_params=pltpu.CompilerParams(
             collective_id=0, has_side_effects=True, vmem_limit_bytes=40 * 1024 * 1024
         ),
-    )(
-        grad_out.reshape(n, width), inputs.reshape(n, width), filt,
-        jnp.asarray(high), jnp.asarray(low),
-    )
+    )(*(
+        pltpu.with_memory_space_constraint(a, pltpu.HBM)
+        for a in (
+            grad_out.reshape(n, width), inputs.reshape(n, width), filt,
+            jnp.asarray(high), jnp.asarray(low),
+        )
+    ))
     return dx.reshape(grad_out.shape), h
 
 

time: 22.8 us -> 18.1 us (0.79)
  local copies, waits for them, and re-layouts: 5.97 us -> 1.36 us
    unnamed x12 -> x2, local copies, waits for them, and re-layouts: 5.97 us -> 1.36 us
where the time goes in v2:
time: 18.1 us; the launch traced here: 17.8 us
  Pallas kernels  15.8 us (87%)
  local copies, waits for them, and re-layouts  1.36 us (8%)
  between operations  0.64 us (4%)
    pallas_call x1, Pallas kernels, fused_body(): pl.pallas_call(functools.partial(kernel, n_ctx, n_dp), out_shape=(jax.Sha...  15.8 us
    unnamed x2, local copies, waits for them, and re-layouts  1.36 us

profile of v2, /device:TPU:0, one launch (start us, length us, event | category | flops | bytes accessed | tf_op | source)
XLA Modules:
  0.0 17.8 jit_solution(13205097192720397627)
XLA Ops:
  0.6 15.8 %shard_map.68 = (bf16[256,256]{1,0:T(8,128)(2,1)S(1)}, f32[256,256]{1,0:T(8,128)S(1)}) custom-call(bf16[256,256]{1,0:T(8,128)(2,1)} %bitcast.4, bf16[256,256]{1,0:T(8,128)(2,1)} %bitcast.5, bf16[256,256]{1,0:T(8,128)(2,1)} %f_hbm.1, bf16[256,512]{1,0:T(8,128)(2,1)} %constant.4.clone.wh_hbm, bf16[256,512]{1,0:T(8,128)(2,1)} %constant.5.clone.wl_hbm), custom_call_target="tpu_custom_call" | custom-call | tf_op jit(solution)/shard_map/pallas_call | solution.py:247
  16.4 0.7 %copy.9 = bf16[1,256,256]{2,1,0:T(8,128)(2,1)} copy(bf16[1,256,256]{2,1,0:T(8,128)(2,1)S(1)} %bitcast.3) | data formatting | bytes 262144
  17.1 0.7 %copy.10 = f32[256,256]{1,0:T(8,128)} copy(f32[256,256]{1,0:T(8,128)S(1)} %get-tuple-element.9) | data formatting | bytes 524288

commit v3 on v2

--- a/solution.py
+++ b/solution.py
@@ -97,38 +97,50 @@
         lanes = pl.ds(pl.multiple_of(c * part, part), part)
         return src[:, lanes].T.reshape(n_dp, cb, n)
 
-    for i, src in enumerate((g_in, x_in)):
-        loads[i].wait()
-    for dc in range(n_ctx - 1, -1, -1):
+    def spread_out(sig, src, dc):
         pc, _ = ahead(dc, 0)
-        blocks = pl.ds(pc * n_dp, n_dp)
-        out1[blocks, 0] = turn(g_in, pc)
-        out1[blocks, 1] = turn(x_in, pc)
-        if dc == n_ctx - 1:
+        out1[sig, pl.ds(pc * n_dp, n_dp)] = turn(src, pc)
+        if sig == 0 and dc == n_ctx - 1:
             pl.semaphore_wait(barrier, group - 1)
         for dd in range(n_dp - 1, -1, -1):
             if (dc, dd) != (0, 0):
                 _, pd = ahead(dc, dd)
                 peer = pc * n_dp + pd
-                push(out1.at[peer], in1.at[ctx, dp], send1.at[peer], recv1.at[me], pc, pd)
+                push(
+                    out1.at[sig, peer], in1.at[sig, ctx, dp],
+                    send1.at[sig, peer], recv1.at[sig, me], pc, pd,
+                )
+
+    loads[0].wait()
+    for dc in range(n_ctx - 1, 0, -1):
+        spread_out(0, g_in, dc)
     loads[2].wait()
-    outf[...] = f_in[...].T.reshape(group, cb, n)
-    for dc in range(1, n_ctx):
+    for dc in range(n_ctx - 1, 0, -1):
         pc, _ = ahead(dc, 0)
+        outf[pl.ds(pc * n_dp, n_dp)] = turn(f_in, pc)
         push(outf.at[pc * n_dp + dp], inf.at[ctx], sendf.at[dc], recvf.at[ctx], pc, dp)
-    in1[ctx, dp] = out1[me]
+    spread_out(0, g_in, 0)
+    loads[1].wait()
+    for dc in range(n_ctx - 1, -1, -1):
+        spread_out(1, x_in, dc)
+    outf[pl.ds(ctx * n_dp, n_dp)] = turn(f_in, ctx)
+    in1[0, ctx, dp] = out1[0, me]
+    in1[1, ctx, dp] = out1[1, me]
     inf[ctx] = outf[me]
     loads[3].wait()
     loads[4].wait()
 
-    for dc in range(n_ctx):
+    def collect(sig, dc):
         sc, _ = behind(dc, 0)
         for dd in range(n_dp):
             if (dc, dd) != (0, 0):
                 _, sd = behind(dc, dd)
-                arrived(out1.at[me], in1.at[sc, sd], send1.at[me], recv1.at[sc * n_dp + sd], sc, sd)
-        rows = in1[sc].reshape(n_dp * 2 * cb, n)
-        spec[sc] = (dot(rows, wh[...]) + dot(rows, wl[...])).reshape(n_dp, 2, cb, 2 * n)
+                arrived(
+                    out1.at[sig, me], in1.at[sig, sc, sd],
+                    send1.at[sig, me], recv1.at[sig, sc * n_dp + sd], sc, sd,
+                )
+        rows = in1[sig, sc].reshape(part, n)
+        spec[sig, sc] = (dot(rows, wh[...]) + dot(rows, wl[...])).reshape(n_dp, cb, 2 * n)
 
     def put(row, lanes, value):
         high = value.astype(jnp.bfloat16)
@@ -136,8 +148,8 @@
         s_lo[pl.ds(row, cb), lanes] = (value - high.astype(jnp.float32)).astype(jnp.bfloat16)
 
     def shifted(parity, b, re, im):
-        g0r, g0i = spec[0, b, 0, :, re], spec[0, b, 0, :, im]
-        g1r, g1i = spec[1, b, 0, :, re], spec[1, b, 0, :, im]
+        g0r, g0i = spec[0, 0, b, :, re], spec[0, 0, b, :, im]
+        g1r, g1i = spec[0, 1, b, :, re], spec[0, 1, b, :, im]
         if parity == 0:
             return g0r + g1i, g0i - g1r, g1r, g1i
         return g0r - g1i, g0i + g1r, g1r, g1i
@@ -151,35 +163,14 @@
         total = dot_nt(high, wh[...]) + (dot_nt(low, wh[...]) + dot_nt(high, wl[...]))
         return total * (1.0 / n)
 
-    for parity in range(2):
-        re, im = lanes_of(parity)
-        h0r = h0i = h1r = h1i = jnp.zeros((cb, half_lanes), jnp.float32)
-        for b in range(n_dp):
-            qr, qi, g1r, g1i = shifted(parity, b, re, im)
-            x0r, x0i = spec[0, b, 1, :, re], spec[0, b, 1, :, im]
-            x1r, x1i = spec[1, b, 1, :, re], spec[1, b, 1, :, im]
-            ar, ai = corr(x0r, x0i, qr, qi)
-            br, bi = corr(x1r, x1i, g1r, g1i)
-            cr, ci = corr(x0r, x0i, g1r, g1i)
-            h0r, h0i = h0r + (ar + br), h0i + (ai + bi)
-            h1r, h1i = h1r + cr, h1i + ci
-        put(0, re, h0r)
-        put(0, im, h0i)
-        put(cb, re, h1r)
-        put(cb, im, h1i)
-    h_out[...] = inverse(0, n_ctx * cb).reshape(h_out.shape)
-    for dc, dd in remote:
-        if dd % 2 == 0:
-            pc, pd = ahead(dc, dd)
-            push(h_out.at[pc], h_in.at[me], send_h.at[pc * n_dp + pd], recv_h.at[me], pc, pd)
-    push(h_out.at[ctx], h_in.at[me], send_h.at[ctx * n_dp + sib], recv_h.at[me], ctx, sib)
-    h_in[me] = h_out[ctx]
-
+    collect(0, 0)
     for dc in range(1, n_ctx):
         sc, _ = behind(dc, 0)
         arrived(outf.at[me], inf.at[sc], sendf.at[0], recvf.at[sc], sc, dp)
     rows_f = inf[...].reshape(n_ctx * cb, n)
     specf[...] = (dot(rows_f, wh[...]) + dot(rows_f, wl[...])).reshape(specf.shape)
+    for dc in range(1, n_ctx):
+        collect(0, dc)
     first = n_ctx * cb
     for parity in range(2):
         re, im = lanes_of(parity)
@@ -205,6 +196,32 @@
                 push(dx_out.at[pc, pd], dx_in.at[me], send_dx.at[pc * n_dp + pd], recv_dx.at[me], pc, pd)
     dx_in[me] = dx_out[ctx, dp]
 
+    for dc in range(n_ctx):
+        collect(1, dc)
+    for parity in range(2):
+        re, im = lanes_of(parity)
+        h0r = h0i = h1r = h1i = jnp.zeros((cb, half_lanes), jnp.float32)
+        for b in range(n_dp):
+            qr, qi, g1r, g1i = shifted(parity, b, re, im)
+            x0r, x0i = spec[1, 0, b, :, re], spec[1, 0, b, :, im]
+            x1r, x1i = spec[1, 1, b, :, re], spec[1, 1, b, :, im]
+            ar, ai = corr(x0r, x0i, qr, qi)
+            br, bi = corr(x1r, x1i, g1r, g1i)
+            cr, ci = corr(x0r, x0i, g1r, g1i)
+            h0r, h0i = h0r + (ar + br), h0i + (ai + bi)
+            h1r, h1i = h1r + cr, h1i + ci
+        put(0, re, h0r)
+        put(0, im, h0i)
+        put(cb, re, h1r)
+        put(cb, im, h1i)
+    h_out[...] = inverse(0, n_ctx * cb).reshape(h_out.shape)
+    for dc, dd in remote:
+        if dd % 2 == 0:
+            pc, pd = ahead(dc, dd)
+            push(h_out.at[pc], h_in.at[me], send_h.at[pc * n_dp + pd], recv_h.at[me], pc, pd)
+    push(h_out.at[ctx], h_in.at[me], send_h.at[ctx * n_dp + sib], recv_h.at[me], ctx, sib)
+    h_in[me] = h_out[ctx]
+
     def h_arrived(sc, sd):
         source = sc * n_dp + sd
         arrived(h_out.at[0], h_in.at[source], send_h.at[me], recv_h.at[source], sc, sd)
@@ -219,10 +236,6 @@
             if (dc, dd) != (0, 0):
                 source = h_arrived(*behind(dc, dd))
                 push(h_in.at[source], h_in.at[source], send_f.at[source], recv_h.at[source], ctx, sib)
-    for dc in range(n_ctx):
-        for dd in range(1, n_dp, 2):
-            h_arrived(*behind(dc, dd))
-        finish(behind(dc, 0)[0], h_in, h_ref)
     for dc in range(n_ctx):
         sc, _ = behind(dc, 0)
         for dd in range(n_dp):
@@ -231,6 +244,10 @@
                 source = sc * n_dp + sd
                 arrived(dx_out.at[0, 0], dx_in.at[source], send_dx.at[me], recv_dx.at[source], sc, sd)
         finish(sc, dx_in, dx_ref)
+    for dc in range(n_ctx):
+        for dd in range(1, n_dp, 2):
+            h_arrived(*behind(dc, dd))
+        finish(behind(dc, 0)[0], h_in, h_ref)
     for c in sent:
         c.wait_send()
 
@@ -258,11 +275,11 @@
             pltpu.VMEM((n, width), bf16),
             pltpu.VMEM((n, 2 * n), bf16),
             pltpu.VMEM((n, 2 * n), bf16),
-            pltpu.VMEM((group, 2, cb, n), bf16),
+            pltpu.VMEM((2, group, cb, n), bf16),
             pltpu.VMEM((group, cb, n), bf16),
-            pltpu.VMEM((n_ctx, n_dp, 2, cb, n), bf16),
+            pltpu.VMEM((2, n_ctx, n_dp, cb, n), bf16),
             pltpu.VMEM((n_ctx, cb, n), bf16),
-            pltpu.VMEM((n_ctx, n_dp, 2, cb, 2 * n), f32),
+            pltpu.VMEM((2, n_ctx, n_dp, cb, 2 * n), f32),
             pltpu.VMEM((n_ctx, cb, 2 * n), f32),
             pltpu.VMEM((n_ctx * cb + group * cb, 2 * n), bf16),
             pltpu.VMEM((n_ctx * cb + group * cb, 2 * n), bf16),
@@ -271,7 +288,7 @@
             pltpu.VMEM((group, cb, n), f32),
             pltpu.VMEM((group, cb, n), bf16),
             sems((5,)),
-            sems((group,)), sems((group,)),
+            sems((2, group)), sems((2, group)),
             sems((n_ctx,)), sems((n_ctx,)),
             sems((group,)), sems((group,)), sems((group,)),
             sems((group,)), sems((group,)),

time: 18.1 us -> 17.9 us (0.989)
  no operation moved by 1% of the time
where the time goes in v3:
time: 17.9 us; the launch traced here: 17.7 us
  Pallas kernels  15.7 us (88%)
  local copies, waits for them, and re-layouts  1.36 us (8%)
  between operations  0.64 us (4%)
    pallas_call x1, Pallas kernels, fused_body(): pl.pallas_call(functools.partial(kernel, n_ctx, n_dp), out_shape=(jax.Sha...  15.7 us
    unnamed x2, local copies, waits for them, and re-layouts  1.36 us

profile of v3, /device:TPU:0, one launch (start us, length us, event | category | flops | bytes accessed | tf_op | source)
XLA Modules:
  0.0 17.7 jit_solution(2760262108247257625)
XLA Ops:
  0.6 15.7 %shard_map.68 = (bf16[256,256]{1,0:T(8,128)(2,1)S(1)}, f32[256,256]{1,0:T(8,128)S(1)}) custom-call(bf16[256,256]{1,0:T(8,128)(2,1)} %bitcast.4, bf16[256,256]{1,0:T(8,128)(2,1)} %bitcast.5, bf16[256,256]{1,0:T(8,128)(2,1)} %f_hbm.1, bf16[256,512]{1,0:T(8,128)(2,1)} %constant.4.clone.wh_hbm, bf16[256,512]{1,0:T(8,128)(2,1)} %constant.5.clone.wl_hbm), custom_call_target="tpu_custom_call" | custom-call | tf_op jit(solution)/shard_map/pallas_call | solution.py:264
  16.3 0.7 %copy.9 = bf16[1,256,256]{2,1,0:T(8,128)(2,1)} copy(bf16[1,256,256]{2,1,0:T(8,128)(2,1)S(1)} %bitcast.3) | data formatting | bytes 262144
  17.0 0.7 %copy.10 = f32[256,256]{1,0:T(8,128)} copy(f32[256,256]{1,0:T(8,128)S(1)} %get-tuple-element.9) | data formatting | bytes 524288

commit v4 on v3

--- a/solution.py
+++ b/solution.py
@@ -42,7 +42,7 @@
     dx_ref, h_ref,
     g_in, x_in, f_in, wh, wl,
     out1, outf, in1, inf, spec, specf, s_hi, s_lo, h_out, dx_out, h_in, dx_in,
-    load_sem, send1, recv1, sendf, recvf, send_h, recv_h, send_f, send_dx, recv_dx,
+    load_sem, send1, recv1, sendf, recvf, send_h, recv_h, recv_f, send_dx, recv_dx,
 ):
     n, width = g_hbm.shape
     group = n_ctx * n_dp
@@ -75,7 +75,6 @@
         c.start()
 
     sib = dp + 1 - 2 * lax.rem(dp, 2)
-    sent = []
 
     def push(src, dst, send, recv, pc, pd):
         c = pltpu.make_async_remote_copy(
@@ -83,13 +82,18 @@
             device_id={"context": pc, "dp": pd}, device_id_type=MESH,
         )
         c.start()
-        sent.append(c)
-
-    def arrived(src, dst, send, recv, pc, pd):
-        pltpu.make_async_remote_copy(
-            src_ref=src, dst_ref=dst, send_sem=send, recv_sem=recv,
-            device_id={"context": pc, "dp": pd}, device_id_type=MESH,
-        ).wait_recv()
+
+    def waiter(ref, sem):
+        return pltpu.make_async_remote_copy(
+            src_ref=ref, dst_ref=ref, send_sem=sem, recv_sem=sem,
+            device_id={"context": ctx, "dp": sib}, device_id_type=MESH,
+        )
+
+    def arrived(ref, sem):
+        waiter(ref, sem).wait_recv()
+
+    def left(ref, sem):
+        waiter(ref, sem).wait_send()
 
     part = n_dp * cb
 
@@ -105,10 +109,9 @@
         for dd in range(n_dp - 1, -1, -1):
             if (dc, dd) != (0, 0):
                 _, pd = ahead(dc, dd)
-                peer = pc * n_dp + pd
                 push(
-                    out1.at[sig, peer], in1.at[sig, ctx, dp],
-                    send1.at[sig, peer], recv1.at[sig, me], pc, pd,
+                    out1.at[sig, pc * n_dp + pd], in1.at[sig, ctx, dp],
+                    send1.at[sig], recv1.at[sig, ctx], pc, pd,
                 )
 
     loads[0].wait()
@@ -132,13 +135,8 @@
 
     def collect(sig, dc):
         sc, _ = behind(dc, 0)
-        for dd in range(n_dp):
-            if (dc, dd) != (0, 0):
-                _, sd = behind(dc, dd)
-                arrived(
-                    out1.at[sig, me], in1.at[sig, sc, sd],
-                    send1.at[sig, me], recv1.at[sig, sc * n_dp + sd], sc, sd,
-                )
+        count = n_dp if dc else n_dp - 1
+        arrived(in1.at[sig, sc, pl.ds(0, count)], recv1.at[sig, sc])
         rows = in1[sig, sc].reshape(part, n)
         spec[sig, sc] = (dot(rows, wh[...]) + dot(rows, wl[...])).reshape(n_dp, cb, 2 * n)
 
@@ -166,7 +164,7 @@
     collect(0, 0)
     for dc in range(1, n_ctx):
         sc, _ = behind(dc, 0)
-        arrived(outf.at[me], inf.at[sc], sendf.at[0], recvf.at[sc], sc, dp)
+        arrived(inf.at[sc], recvf.at[sc])
     rows_f = inf[...].reshape(n_ctx * cb, n)
     specf[...] = (dot(rows_f, wh[...]) + dot(rows_f, wl[...])).reshape(specf.shape)
     for dc in range(1, n_ctx):
@@ -193,7 +191,7 @@
         for dd in range(n_dp - 1, -1, -1):
             if (dc, dd) != (0, 0):
                 _, pd = ahead(dc, dd)
-                push(dx_out.at[pc, pd], dx_in.at[me], send_dx.at[pc * n_dp + pd], recv_dx.at[me], pc, pd)
+                push(dx_out.at[pc, pd], dx_in.at[me], send_dx.at[0], recv_dx.at[ctx], pc, pd)
     dx_in[me] = dx_out[ctx, dp]
 
     for dc in range(n_ctx):
@@ -218,14 +216,9 @@
     for dc, dd in remote:
         if dd % 2 == 0:
             pc, pd = ahead(dc, dd)
-            push(h_out.at[pc], h_in.at[me], send_h.at[pc * n_dp + pd], recv_h.at[me], pc, pd)
-    push(h_out.at[ctx], h_in.at[me], send_h.at[ctx * n_dp + sib], recv_h.at[me], ctx, sib)
+            push(h_out.at[pc], h_in.at[me], send_h.at[0], recv_h.at[ctx, dd // 2], pc, pd)
+    push(h_out.at[ctx], h_in.at[me], send_h.at[0], recv_f.at[ctx], ctx, sib)
     h_in[me] = h_out[ctx]
-
-    def h_arrived(sc, sd):
-        source = sc * n_dp + sd
-        arrived(h_out.at[0], h_in.at[source], send_h.at[me], recv_h.at[source], sc, sd)
-        return source
 
     def finish(sc, src, dst):
         lanes = pl.ds(pl.multiple_of(sc * part, part), part)
@@ -234,22 +227,36 @@
     for dc in range(n_ctx):
         for dd in range(0, n_dp, 2):
             if (dc, dd) != (0, 0):
-                source = h_arrived(*behind(dc, dd))
-                push(h_in.at[source], h_in.at[source], send_f.at[source], recv_h.at[source], ctx, sib)
+                sc, sd = behind(dc, dd)
+                source = sc * n_dp + sd
+                arrived(h_in.at[source], recv_h.at[sc, dd // 2])
+                push(h_in.at[source], h_in.at[source], send_h.at[0], recv_f.at[sc], ctx, sib)
     for dc in range(n_ctx):
         sc, _ = behind(dc, 0)
-        for dd in range(n_dp):
-            if (dc, dd) != (0, 0):
-                _, sd = behind(dc, dd)
-                source = sc * n_dp + sd
-                arrived(dx_out.at[0, 0], dx_in.at[source], send_dx.at[me], recv_dx.at[source], sc, sd)
+        count = n_dp if dc else n_dp - 1
+        arrived(dx_in.at[pl.ds(0, count)], recv_dx.at[sc])
         finish(sc, dx_in, dx_ref)
     for dc in range(n_ctx):
-        for dd in range(1, n_dp, 2):
-            h_arrived(*behind(dc, dd))
-        finish(behind(dc, 0)[0], h_in, h_ref)
-    for c in sent:
-        c.wait_send()
+        sc, _ = behind(dc, 0)
+        arrived(h_in.at[pl.ds(0, n_dp // 2)], recv_f.at[sc])
+        finish(sc, h_in, h_ref)
+    for sig in range(2):
+        left(out1.at[sig, pl.ds(0, group - 1)], send1.at[sig])
+    for dc in range(1, n_ctx):
+        left(inf.at[0], sendf.at[dc])
+    left(dx_in.at[pl.ds(0, group - 1)], send_dx.at[0])
+    left(h_in.at[pl.ds(0, group - 1)], send_h.at[0])
+
+
+def write_out(dx_src, h_src, dx_ref, h_ref, sem):
+    copies = [
+        pltpu.make_async_copy(h_src, h_ref, sem.at[0]),
+        pltpu.make_async_copy(dx_src, dx_ref, sem.at[1]),
+    ]
+    for c in copies:
+        c.start()
+    for c in copies:
+        c.wait()
 
 
 def fused_body(n_ctx, n_dp, grad_out, inputs, filt):
@@ -288,10 +295,10 @@
             pltpu.VMEM((group, cb, n), f32),
             pltpu.VMEM((group, cb, n), bf16),
             sems((5,)),
-            sems((2, group)), sems((2, group)),
+            sems((2,)), sems((2, n_ctx)),
             sems((n_ctx,)), sems((n_ctx,)),
-            sems((group,)), sems((group,)), sems((group,)),
-            sems((group,)), sems((group,)),
+            sems((1,)), sems((n_ctx, n_dp // 2)), sems((n_ctx,)),
+            sems((1,)), sems((n_ctx,)),
         ],
         compiler_params=pltpu.CompilerParams(
             collective_id=0, has_side_effects=True, vmem_limit_bytes=40 * 1024 * 1024
@@ -303,6 +310,13 @@
             jnp.asarray(high), jnp.asarray(low),
         )
     ))
+    dx, h = pl.pallas_call(
+        write_out,
+        out_shape=(pltpu.HBM((n, width), bf16), pltpu.HBM((n, width), f32)),
+        in_specs=[pl.BlockSpec(memory_space=pl.ANY)] * 2,
+        out_specs=(hbm_spec, hbm_spec),
+        scratch_shapes=[sems((2,))],
+    )(dx, h)
     return dx.reshape(grad_out.shape), h
 
 

time: 17.9 us -> 30.3 us (1.69)
  Pallas kernels: 15.7 us -> 28.2 us
    pallas_call x0 -> x1, Pallas kernels: none -> 13 us  [fused_body(): pl.pallas_call(write_out, out_shape=(pltpu.HBM((n, width), bf16), pltpu.H...]
    pallas_call x1, Pallas kernels: 15.7 us -> 15.1 us  [fused_body(): pl.pallas_call(functools.partial(kernel, n_ctx, n_dp), out_shape=(jax.Sha...]
    unnamed x2 -> x4, local copies, waits for them, and re-layouts: 1.36 us -> 1.34 us
where the time goes in v4:
time: 30.3 us; the launch traced here: 30.2 us
  Pallas kernels  28.2 us (93%)
  local copies, waits for them, and re-layouts  1.34 us (4%)
  between operations  0.65 us (2%)
    pallas_call x1, Pallas kernels, fused_body(): pl.pallas_call(functools.partial(kernel, n_ctx, n_dp), out_shape=(jax.Sha...  15.1 us
    pallas_call x1, Pallas kernels, fused_body(): pl.pallas_call(write_out, out_shape=(pltpu.HBM((n, width), bf16), pltpu.H...  13 us
    unnamed x4, local copies, waits for them, and re-layouts  1.34 us

profile of v4, /device:TPU:0, one launch (start us, length us, event | category | flops | bytes accessed | tf_op | source)
XLA Modules:
  0.0 30.2 jit_solution(11917436469938279626)
XLA Ops:
  0.6 15.1 %shard_map.68 = (bf16[256,256]{1,0:T(8,128)(2,1)S(1)}, f32[256,256]{1,0:T(8,128)S(1)}) custom-call(bf16[256,256]{1,0:T(8,128)(2,1)} %bitcast.3, bf16[256,256]{1,0:T(8,128)(2,1)} %bitcast.4, bf16[256,256]{1,0:T(8,128)(2,1)} %f_hbm.1, bf16[256,512]{1,0:T(8,128)(2,1)} %constant.4.clone.wh_hbm, bf16[256,512]{1,0:T(8,128)(2,1)} %constant.5.clone.wl_hbm), custom_call_target="tpu_custom_call" | custom-call | tf_op jit(solution)/shard_map/pallas_call | solution.py:271
  15.8 0.0 copy-start
  15.8 0.7 %copy-done = f32[256,256]{1,0:T(8,128)} copy-done((f32[256,256]{1,0:T(8,128)}, f32[256,256]{1,0:T(8,128)S(1)}, u32[]{:S(2)}) %copy-start) | copy-done | bytes 262168
  16.5 0.0 copy-start.1
  16.5 0.7 %copy-done.1 = bf16[256,256]{1,0:T(8,128)(2,1)} copy-done((bf16[256,256]{1,0:T(8,128)(2,1)}, bf16[256,256]{1,0:T(8,128)(2,1)S(1)}, u32[]{:S(2)}) %copy-start.1) | copy-done | bytes 131096
  17.1 13.0 %shard_map.69 = (bf16[256,256]{1,0:T(8,128)(2,1)}, f32[256,256]{1,0:T(8,128)}) custom-call(bf16[256,256]{1,0:T(8,128)(2,1)} %copy-done.1, f32[256,256]{1,0:T(8,128)} %copy-done), custom_call_target="tpu_custom_call" | custom-call | tf_op jit(solution)/shard_map/pallas_call | solution.py:313
Async XLA Ops:
  15.8 0.7 %copy-start = (f32[256,256]{1,0:T(8,128)}, f32[256,256]{1,0:T(8,128)S(1)}, u32[]{:S(2)}) copy-start(f32[256,256]{1,0:T(8,128)S(1)} %get-tuple-element.7.h_src) | copy-start | bytes 786436
  16.5 0.7 %copy-start.1 = (bf16[256,256]{1,0:T(8,128)(2,1)}, bf16[256,256]{1,0:T(8,128)(2,1)S(1)}, u32[]{:S(2)}) copy-start(bf16[256,256]{1,0:T(8,128)(2,1)S(1)} %get-tuple-element.6.dx_src) | copy-start | bytes 393220

commit v5 on v4

--- a/solution.py
+++ b/solution.py
@@ -11,7 +11,6 @@
 from jax.sharding import PartitionSpec as P
 
 MESH = pl.DeviceIdType.MESH
-NT = (((1,), (1,)), ((), ()))
 
 
 def half_step_table(n):
@@ -28,19 +27,15 @@
     return jnp.dot(a, b, preferred_element_type=jnp.float32)
 
 
-def dot_nt(a, b):
-    return lax.dot_general(a, b, NT, preferred_element_type=jnp.float32)
-
-
 def corr(fr, fi, gr, gi):
     return fr * gr + fi * gi, fr * gi - fi * gr
 
 
 def kernel(
     n_ctx, n_dp,
-    g_hbm, x_hbm, f_hbm, wh_hbm, wl_hbm,
+    g_hbm, x_hbm, f_hbm, wh_hbm, wl_hbm, vh_hbm, vl_hbm,
     dx_ref, h_ref,
-    g_in, x_in, f_in, wh, wl,
+    g_in, x_in, f_in, wh, wl, vh, vl,
     out1, outf, in1, inf, spec, specf, s_hi, s_lo, h_out, dx_out, h_in, dx_in,
     load_sem, send1, recv1, sendf, recvf, send_h, recv_h, recv_f, send_dx, recv_dx,
 ):
@@ -68,7 +63,10 @@
     loads = [
         pltpu.make_async_copy(src, dst, load_sem.at[i])
         for i, (src, dst) in enumerate(
-            [(g_hbm, g_in), (x_hbm, x_in), (f_hbm, f_in), (wh_hbm, wh), (wl_hbm, wl)]
+            [
+                (g_hbm, g_in), (x_hbm, x_in), (f_hbm, f_in), (wh_hbm, wh), (wl_hbm, wl),
+                (vh_hbm, vh), (vl_hbm, vl),
+            ]
         )
     ]
     for c in loads:
@@ -132,6 +130,8 @@
     inf[ctx] = outf[me]
     loads[3].wait()
     loads[4].wait()
+    loads[5].wait()
+    loads[6].wait()
 
     def collect(sig, dc):
         sc, _ = behind(dc, 0)
@@ -158,7 +158,7 @@
     def inverse(start, size):
         rows = pl.ds(start, size)
         high, low = s_hi[rows, :], s_lo[rows, :]
-        total = dot_nt(high, wh[...]) + (dot_nt(low, wh[...]) + dot_nt(high, wl[...]))
+        total = dot(high, vh[...]) + (dot(low, vh[...]) + dot(high, vl[...]))
         return total * (1.0 / n)
 
     collect(0, 0)
@@ -274,7 +274,7 @@
             jax.ShapeDtypeStruct((n, width), bf16),
             jax.ShapeDtypeStruct((n, width), f32),
         ),
-        in_specs=[hbm_spec] * 5,
+        in_specs=[hbm_spec] * 7,
         out_specs=(vmem_spec, vmem_spec),
         scratch_shapes=[
             pltpu.VMEM((n, width), bf16),
@@ -282,6 +282,8 @@
             pltpu.VMEM((n, width), bf16),
             pltpu.VMEM((n, 2 * n), bf16),
             pltpu.VMEM((n, 2 * n), bf16),
+            pltpu.VMEM((2 * n, n), bf16),
+            pltpu.VMEM((2 * n, n), bf16),
             pltpu.VMEM((2, group, cb, n), bf16),
             pltpu.VMEM((group, cb, n), bf16),
             pltpu.VMEM((2, n_ctx, n_dp, cb, n), bf16),
@@ -294,7 +296,7 @@
             pltpu.VMEM((n_ctx, n_dp, cb, n), bf16),
             pltpu.VMEM((group, cb, n), f32),
             pltpu.VMEM((group, cb, n), bf16),
-            sems((5,)),
+            sems((7,)),
             sems((2,)), sems((2, n_ctx)),
             sems((n_ctx,)), sems((n_ctx,)),
             sems((1,)), sems((n_ctx, n_dp // 2)), sems((n_ctx,)),
@@ -308,6 +310,7 @@
         for a in (
             grad_out.reshape(n, width), inputs.reshape(n, width), filt,
             jnp.asarray(high), jnp.asarray(low),
+            jnp.asarray(np.ascontiguousarray(high.T)), jnp.asarray(np.ascontiguousarray(low.T)),
         )
     ))
     dx, h = pl.pallas_call(
@@ -316,6 +319,7 @@
         in_specs=[pl.BlockSpec(memory_space=pl.ANY)] * 2,
         out_specs=(hbm_spec, hbm_spec),
         scratch_shapes=[sems((2,))],
+        compiler_params=pltpu.CompilerParams(vmem_limit_bytes=4 * 1024 * 1024),
     )(dx, h)
     return dx.reshape(grad_out.shape), h
 

time: 30.3 us -> 16.6 us (0.55)
  Pallas kernels: 28.2 us -> 15.8 us
  local copies, waits for them, and re-layouts: 1.34 us -> 0 us
    pallas_call x1, Pallas kernels: 13 us -> 0.76 us  [fused_body(): pl.pallas_call(write_out, out_shape=(pltpu.HBM((n, width), bf16), pltpu.H...]
    unnamed x4 -> x0, local copies, waits for them, and re-layouts: 1.34 us -> none
where the time goes in v5:
time: 16.6 us; the launch traced here: 16.4 us
  Pallas kernels  15.8 us (95%)
  between operations  0.64 us (4%)
    pallas_call x1, Pallas kernels, fused_body(): pl.pallas_call(functools.partial(kernel, n_ctx, n_dp), out_shape=(jax.Sha...  15 us
    pallas_call x1, Pallas kernels, fused_body(): pl.pallas_call(write_out, out_shape=(pltpu.HBM((n, width), bf16), pltpu.H...  0.76 us

profile of v5, /device:TPU:0, one launch (start us, length us, event | category | flops | bytes accessed | tf_op | source)
XLA Modules:
  0.0 16.4 jit_solution(14858293306963262313)
XLA Ops:
  0.6 15.0 %shard_map.86 = (bf16[256,256]{1,0:T(8,128)(2,1)S(1)}, f32[256,256]{1,0:T(8,128)S(1)}) custom-call(bf16[256,256]{1,0:T(8,128)(2,1)} %bitcast.3, bf16[256,256]{1,0:T(8,128)(2,1)} %bitcast.4, bf16[256,256]{1,0:T(8,128)(2,1)} %f_hbm.1, bf16[256,512]{1,0:T(8,128)(2,1)} %constant.8.clone.wh_hbm, bf16[256,512]{1,0:T(8,128)(2,1)} %constant.9.clone.wl_hbm, ...), custom_call_target="tpu_custom_call" | custom-call | tf_op jit(solution)/shard_map/pallas_call | solution.py:271
  15.6 0.8 %shard_map.87 = (bf16[256,256]{1,0:T(8,128)(2,1)}, f32[256,256]{1,0:T(8,128)}) custom-call(bf16[256,256]{1,0:T(8,128)(2,1)S(1)} %get-tuple-element.6.dx_src, f32[256,256]{1,0:T(8,128)S(1)} %get-tuple-element.7.h_src), custom_call_target="tpu_custom_call" | custom-call | tf_op jit(solution)/shard_map/pallas_call | solution.py:316

commit v6 on v5

--- a/solution.py
+++ b/solution.py
@@ -99,46 +99,41 @@
         lanes = pl.ds(pl.multiple_of(c * part, part), part)
         return src[:, lanes].T.reshape(n_dp, cb, n)
 
-    def spread_out(sig, src, dc):
+    loads[0].wait()
+    loads[1].wait()
+    for dc in range(n_ctx - 1, -1, -1):
         pc, _ = ahead(dc, 0)
-        out1[sig, pl.ds(pc * n_dp, n_dp)] = turn(src, pc)
-        if sig == 0 and dc == n_ctx - 1:
+        blocks = pl.ds(pc * n_dp, n_dp)
+        out1[blocks, 0] = turn(g_in, pc)
+        out1[blocks, 1] = turn(x_in, pc)
+        if dc == n_ctx - 1:
             pl.semaphore_wait(barrier, group - 1)
         for dd in range(n_dp - 1, -1, -1):
             if (dc, dd) != (0, 0):
                 _, pd = ahead(dc, dd)
                 push(
-                    out1.at[sig, pc * n_dp + pd], in1.at[sig, ctx, dp],
-                    send1.at[sig], recv1.at[sig, ctx], pc, pd,
+                    out1.at[pc * n_dp + pd], in1.at[ctx, dp],
+                    send1.at[0], recv1.at[ctx], pc, pd,
                 )
-
-    loads[0].wait()
-    for dc in range(n_ctx - 1, 0, -1):
-        spread_out(0, g_in, dc)
     loads[2].wait()
     for dc in range(n_ctx - 1, 0, -1):
         pc, _ = ahead(dc, 0)
         outf[pl.ds(pc * n_dp, n_dp)] = turn(f_in, pc)
         push(outf.at[pc * n_dp + dp], inf.at[ctx], sendf.at[dc], recvf.at[ctx], pc, dp)
-    spread_out(0, g_in, 0)
-    loads[1].wait()
-    for dc in range(n_ctx - 1, -1, -1):
-        spread_out(1, x_in, dc)
     outf[pl.ds(ctx * n_dp, n_dp)] = turn(f_in, ctx)
-    in1[0, ctx, dp] = out1[0, me]
-    in1[1, ctx, dp] = out1[1, me]
+    in1[ctx, dp] = out1[me]
     inf[ctx] = outf[me]
     loads[3].wait()
     loads[4].wait()
     loads[5].wait()
     loads[6].wait()
 
-    def collect(sig, dc):
+    def collect(dc):
         sc, _ = behind(dc, 0)
         count = n_dp if dc else n_dp - 1
-        arrived(in1.at[sig, sc, pl.ds(0, count)], recv1.at[sig, sc])
-        rows = in1[sig, sc].reshape(part, n)
-        spec[sig, sc] = (dot(rows, wh[...]) + dot(rows, wl[...])).reshape(n_dp, cb, 2 * n)
+        arrived(in1.at[sc, pl.ds(0, count)], recv1.at[sc])
+        rows = in1[sc].reshape(2 * part, n)
+        spec[sc] = (dot(rows, wh[...]) + dot(rows, wl[...])).reshape(n_dp, 2, cb, 2 * n)
 
     def put(row, lanes, value):
         high = value.astype(jnp.bfloat16)
@@ -146,8 +141,8 @@
         s_lo[pl.ds(row, cb), lanes] = (value - high.astype(jnp.float32)).astype(jnp.bfloat16)
 
     def shifted(parity, b, re, im):
-        g0r, g0i = spec[0, 0, b, :, re], spec[0, 0, b, :, im]
-        g1r, g1i = spec[0, 1, b, :, re], spec[0, 1, b, :, im]
+        g0r, g0i = spec[0, b, 0, :, re], spec[0, b, 0, :, im]
+        g1r, g1i = spec[1, b, 0, :, re], spec[1, b, 0, :, im]
         if parity == 0:
             return g0r + g1i, g0i - g1r, g1r, g1i
         return g0r - g1i, g0i + g1r, g1r, g1i
@@ -161,14 +156,37 @@
         total = dot(high, vh[...]) + (dot(low, vh[...]) + dot(high, vl[...]))
         return total * (1.0 / n)
 
-    collect(0, 0)
+    for dc in range(n_ctx):
+        collect(dc)
+    for parity in range(2):
+        re, im = lanes_of(parity)
+        h0r = h0i = h1r = h1i = jnp.zeros((cb, half_lanes), jnp.float32)
+        for b in range(n_dp):
+            qr, qi, g1r, g1i = shifted(parity, b, re, im)
+            x0r, x0i = spec[0, b, 1, :, re], spec[0, b, 1, :, im]
+            x1r, x1i = spec[1, b, 1, :, re], spec[1, b, 1, :, im]
+            ar, ai = corr(x0r, x0i, qr, qi)
+            br, bi = corr(x1r, x1i, g1r, g1i)
+            cr, ci = corr(x0r, x0i, g1r, g1i)
+            h0r, h0i = h0r + (ar + br), h0i + (ai + bi)
+            h1r, h1i = h1r + cr, h1i + ci
+        put(0, re, h0r)
+        put(0, im, h0i)
+        put(cb, re, h1r)
+        put(cb, im, h1i)
+    h_out[...] = inverse(0, n_ctx * cb).reshape(h_out.shape)
+    for dc, dd in remote:
+        if dd % 2 == 0:
+            pc, pd = ahead(dc, dd)
+            push(h_out.at[pc], h_in.at[me], send_h.at[0], recv_h.at[ctx, dd // 2], pc, pd)
+    push(h_out.at[ctx], h_in.at[me], send_h.at[0], recv_f.at[ctx], ctx, sib)
+    h_in[me] = h_out[ctx]
+
     for dc in range(1, n_ctx):
         sc, _ = behind(dc, 0)
         arrived(inf.at[sc], recvf.at[sc])
     rows_f = inf[...].reshape(n_ctx * cb, n)
     specf[...] = (dot(rows_f, wh[...]) + dot(rows_f, wl[...])).reshape(specf.shape)
-    for dc in range(1, n_ctx):
-        collect(0, dc)
     first = n_ctx * cb
     for parity in range(2):
         re, im = lanes_of(parity)
@@ -194,32 +212,6 @@
                 push(dx_out.at[pc, pd], dx_in.at[me], send_dx.at[0], recv_dx.at[ctx], pc, pd)
     dx_in[me] = dx_out[ctx, dp]
 
-    for dc in range(n_ctx):
-        collect(1, dc)
-    for parity in range(2):
-        re, im = lanes_of(parity)
-        h0r = h0i = h1r = h1i = jnp.zeros((cb, half_lanes), jnp.float32)
-        for b in range(n_dp):
-            qr, qi, g1r, g1i = shifted(parity, b, re, im)
-            x0r, x0i = spec[1, 0, b, :, re], spec[1, 0, b, :, im]
-            x1r, x1i = spec[1, 1, b, :, re], spec[1, 1, b, :, im]
-            ar, ai = corr(x0r, x0i, qr, qi)
-            br, bi = corr(x1r, x1i, g1r, g1i)
-            cr, ci = corr(x0r, x0i, g1r, g1i)
-            h0r, h0i = h0r + (ar + br), h0i + (ai + bi)
-            h1r, h1i = h1r + cr, h1i + ci
-        put(0, re, h0r)
-        put(0, im, h0i)
-        put(cb, re, h1r)
-        put(cb, im, h1i)
-    h_out[...] = inverse(0, n_ctx * cb).reshape(h_out.shape)
-    for dc, dd in remote:
-        if dd % 2 == 0:
-            pc, pd = ahead(dc, dd)
-            push(h_out.at[pc], h_in.at[me], send_h.at[0], recv_h.at[ctx, dd // 2], pc, pd)
-    push(h_out.at[ctx], h_in.at[me], send_h.at[0], recv_f.at[ctx], ctx, sib)
-    h_in[me] = h_out[ctx]
-
     def finish(sc, src, dst):
         lanes = pl.ds(pl.multiple_of(sc * part, part), part)
         dst[:, lanes] = src[pl.ds(sc * n_dp, n_dp)].reshape(part, n).T
@@ -240,8 +232,7 @@
         sc, _ = behind(dc, 0)
         arrived(h_in.at[pl.ds(0, n_dp // 2)], recv_f.at[sc])
         finish(sc, h_in, h_ref)
-    for sig in range(2):
-        left(out1.at[sig, pl.ds(0, group - 1)], send1.at[sig])
+    left(out1.at[pl.ds(0, group - 1)], send1.at[0])
     for dc in range(1, n_ctx):
         left(inf.at[0], sendf.at[dc])
     left(dx_in.at[pl.ds(0, group - 1)], send_dx.at[0])
@@ -284,11 +275,11 @@
             pltpu.VMEM((n, 2 * n), bf16),
             pltpu.VMEM((2 * n, n), bf16),
             pltpu.VMEM((2 * n, n), bf16),
-            pltpu.VMEM((2, group, cb, n), bf16),
+            pltpu.VMEM((group, 2, cb, n), bf16),
             pltpu.VMEM((group, cb, n), bf16),
-            pltpu.VMEM((2, n_ctx, n_dp, cb, n), bf16),
+            pltpu.VMEM((n_ctx, n_dp, 2, cb, n), bf16),
             pltpu.VMEM((n_ctx, cb, n), bf16),
-            pltpu.VMEM((2, n_ctx, n_dp, cb, 2 * n), f32),
+            pltpu.VMEM((n_ctx, n_dp, 2, cb, 2 * n), f32),
             pltpu.VMEM((n_ctx, cb, 2 * n), f32),
             pltpu.VMEM((n_ctx * cb + group * cb, 2 * n), bf16),
             pltpu.VMEM((n_ctx * cb + group * cb, 2 * n), bf16),
@@ -297,7 +288,7 @@
             pltpu.VMEM((group, cb, n), f32),
             pltpu.VMEM((group, cb, n), bf16),
             sems((7,)),
-            sems((2,)), sems((2, n_ctx)),
+            sems((1,)), sems((n_ctx,)),
             sems((n_ctx,)), sems((n_ctx,)),
             sems((1,)), sems((n_ctx, n_dp // 2)), sems((n_ctx,)),
             sems((1,)), sems((n_ctx,)),

time: 16.6 us -> 16.7 us (level)
  no operation moved by 1% of the time
where the time goes in v6:
time: 16.7 us; the launch traced here: 16.6 us
  Pallas kernels  15.9 us (95%)
  between operations  0.64 us (4%)
    pallas_call x1, Pallas kernels, fused_body(): pl.pallas_call(functools.partial(kernel, n_ctx, n_dp), out_shape=(jax.Sha...  15.2 us
    pallas_call x1, Pallas kernels, fused_body(): pl.pallas_call(write_out, out_shape=(pltpu.HBM((n, width), bf16), pltpu.H...  0.76 us

profile of v6, /device:TPU:0, one launch (start us, length us, event | category | flops | bytes accessed | tf_op | source)
XLA Modules:
  0.0 16.6 jit_solution(13825000948635156362)
XLA Ops:
  0.6 15.2 %shard_map.86 = (bf16[256,256]{1,0:T(8,128)(2,1)S(1)}, f32[256,256]{1,0:T(8,128)S(1)}) custom-call(bf16[256,256]{1,0:T(8,128)(2,1)} %bitcast.3, bf16[256,256]{1,0:T(8,128)(2,1)} %bitcast.4, bf16[256,256]{1,0:T(8,128)(2,1)} %f_hbm.1, bf16[256,512]{1,0:T(8,128)(2,1)} %constant.8.clone.wh_hbm, bf16[256,512]{1,0:T(8,128)(2,1)} %constant.9.clone.wl_hbm, ...), custom_call_target="tpu_custom_call" | custom-call | tf_op jit(solution)/shard_map/pallas_call | solution.py:262
  15.8 0.8 %shard_map.87 = (bf16[256,256]{1,0:T(8,128)(2,1)}, f32[256,256]{1,0:T(8,128)}) custom-call(bf16[256,256]{1,0:T(8,128)(2,1)S(1)} %get-tuple-element.6.dx_src, f32[256,256]{1,0:T(8,128)S(1)} %get-tuple-element.7.h_src), custom_call_target="tpu_custom_call" | custom-call | tf_op jit(solution)/shard_map/pallas_call | solution.py:307

commit v7 on v5

--- a/solution.py
+++ b/solution.py
@@ -37,7 +37,7 @@
     dx_ref, h_ref,
     g_in, x_in, f_in, wh, wl, vh, vl,
     out1, outf, in1, inf, spec, specf, s_hi, s_lo, h_out, dx_out, h_in, dx_in,
-    load_sem, send1, recv1, sendf, recvf, send_h, recv_h, recv_f, send_dx, recv_dx,
+    load_sem, send1, recv1, sendf, recvf, send_h, recv_h, send_dx, recv_dx,
 ):
     n, width = g_hbm.shape
     group = n_ctx * n_dp
@@ -213,24 +213,15 @@
         put(cb, re, h1r)
         put(cb, im, h1i)
     h_out[...] = inverse(0, n_ctx * cb).reshape(h_out.shape)
-    for dc, dd in remote:
-        if dd % 2 == 0:
-            pc, pd = ahead(dc, dd)
-            push(h_out.at[pc], h_in.at[me], send_h.at[0], recv_h.at[ctx, dd // 2], pc, pd)
-    push(h_out.at[ctx], h_in.at[me], send_h.at[0], recv_f.at[ctx], ctx, sib)
+    for o in remote:
+        pc, pd = ahead(*o)
+        push(h_out.at[pc], h_in.at[me], send_h.at[0], recv_h.at[ctx], pc, pd)
     h_in[me] = h_out[ctx]
 
     def finish(sc, src, dst):
         lanes = pl.ds(pl.multiple_of(sc * part, part), part)
         dst[:, lanes] = src[pl.ds(sc * n_dp, n_dp)].reshape(part, n).T
 
-    for dc in range(n_ctx):
-        for dd in range(0, n_dp, 2):
-            if (dc, dd) != (0, 0):
-                sc, sd = behind(dc, dd)
-                source = sc * n_dp + sd
-                arrived(h_in.at[source], recv_h.at[sc, dd // 2])
-                push(h_in.at[source], h_in.at[source], send_h.at[0], recv_f.at[sc], ctx, sib)
     for dc in range(n_ctx):
         sc, _ = behind(dc, 0)
         count = n_dp if dc else n_dp - 1
@@ -238,7 +229,8 @@
         finish(sc, dx_in, dx_ref)
     for dc in range(n_ctx):
         sc, _ = behind(dc, 0)
-        arrived(h_in.at[pl.ds(0, n_dp // 2)], recv_f.at[sc])
+        count = n_dp if dc else n_dp - 1
+        arrived(h_in.at[pl.ds(0, count)], recv_h.at[sc])
         finish(sc, h_in, h_ref)
     for sig in range(2):
         left(out1.at[sig, pl.ds(0, group - 1)], send1.at[sig])
@@ -299,7 +291,7 @@
             sems((7,)),
             sems((2,)), sems((2, n_ctx)),
             sems((n_ctx,)), sems((n_ctx,)),
-            sems((1,)), sems((n_ctx, n_dp // 2)), sems((n_ctx,)),
+            sems((1,)), sems((n_ctx,)),
             sems((1,)), sems((n_ctx,)),
         ],
         compiler_params=pltpu.CompilerParams(

time: 16.6 us -> 17.2 us (1.036)
  Pallas kernels: 15.8 us -> 16.4 us
    pallas_call x1, Pallas kernels: 15 us -> 15.6 us  [fused_body(): pl.pallas_call(functools.partial(kernel, n_ctx, n_dp), out_shape=(jax.Sha...]
where the time goes in v7:
time: 17.2 us; the launch traced here: 17 us
  Pallas kernels  16.4 us (95%)
  between operations  0.64 us (4%)
    pallas_call x1, Pallas kernels, fused_body(): pl.pallas_call(functools.partial(kernel, n_ctx, n_dp), out_shape=(jax.Sha...  15.6 us
    pallas_call x1, Pallas kernels, fused_body(): pl.pallas_call(write_out, out_shape=(pltpu.HBM((n, width), bf16), pltpu.H...  0.76 us

profile of v7, /device:TPU:0, one launch (start us, length us, event | category | flops | bytes accessed | tf_op | source)
XLA Modules:
  0.0 17.0 jit_solution(9335207601756825199)
XLA Ops:
  0.6 15.6 %shard_map.86 = (bf16[256,256]{1,0:T(8,128)(2,1)S(1)}, f32[256,256]{1,0:T(8,128)S(1)}) custom-call(bf16[256,256]{1,0:T(8,128)(2,1)} %bitcast.3, bf16[256,256]{1,0:T(8,128)(2,1)} %bitcast.4, bf16[256,256]{1,0:T(8,128)(2,1)} %f_hbm.1, bf16[256,512]{1,0:T(8,128)(2,1)} %constant.8.clone.wh_hbm, bf16[256,512]{1,0:T(8,128)(2,1)} %constant.9.clone.wl_hbm, ...), custom_call_target="tpu_custom_call" | custom-call | tf_op jit(solution)/shard_map/pallas_call | solution.py:263
  16.3 0.8 %shard_map.87 = (bf16[256,256]{1,0:T(8,128)(2,1)}, f32[256,256]{1,0:T(8,128)}) custom-call(bf16[256,256]{1,0:T(8,128)(2,1)S(1)} %get-tuple-element.6.dx_src, f32[256,256]{1,0:T(8,128)S(1)} %get-tuple-element.7.h_src), custom_call_target="tpu_custom_call" | custom-call | tf_op jit(solution)/shard_map/pallas_call | solution.py:308
